TPU v7x, 32 devices: a whole 2x2x4 slice. The times are simulated.
32 devices in a mesh: groups: 2 (over x), vel: 8 (over z, y), sub: 2 (over core).
Axes of the slice: x: 2, y: 2, z: 4, core: 2. Of those that a mesh axis runs over, the one named last changes fastest.
Arguments:
- dist: float32 [16, 256, 1024], P('sub', 'vel', 'groups'), parts along dimension 2, may hold values from 0 to 6, as said below
- cell_type: int32 [1024], P('groups'), parts along dimension 0, may hold values from 0 to 1, as said below
- groove_mask: int32 [64], P('groups'), parts along dimension 0, may hold values 0 or 1
Outputs:
- dist_next: float32 [16, 256, 1024], P('sub', 'vel', 'groups'), parts along dimension 2
There are 2 independent parts, one for each index of `groups`. A program takes and returns all parts, laid end to end along the dimension named above; each array names one. Nothing has to cross between parts.
Inputs may be any that keep to these rules, and one draw needn't show every extreme that they name: `cell_type`: in each column the solid cells are its lowest ones; a column holds at most a quarter of 16 of them, and every draw has columns with that many and columns with none; grooves repeat along the columns with a period of 4 to 12 columns. `dist`: every entry is positive.
All inputs are finite; a program needn't handle non-finite values.
Results may differ from a plain program's by a relative error of at most 0.0001.
Values sent between devices are 32-bit elements; how exact they have to be, the bound alone decides.
A program may use at most 128 MiB of HBM per device.

v0:
```python
import math

import jax
import jax.numpy as jnp
from jax import lax
from jax.sharding import PartitionSpec as P

VN = 16
SY = 16
STEPS = 2


VEL_RANGE = 5.0
TOP_SPEED = 1.0
ACC_LAND = 0.4
ACC_TOP = 0.7
KNUDSEN = 1.0
HIGHEST = lax.Precision.HIGHEST
FORMS = ("kj,jxzc->kxzc", "kj,yjzc->ykzc", "kj,yxjc->yxkc")


def swapped(value, axis, distance):
    mask = 2**distance
    pairs = [(source, source ^ mask) for source in range(lax.axis_size(axis))]
    return lax.ppermute(value, axis, pairs)


def spacing_of(count):
    return 2.0 * VEL_RANGE / count


def time_step(count):
    return 0.8 / ((count - 1) * spacing_of(count))


def speeds(index, count):
    return (index.astype(jnp.float32) - (count - 1) / 2.0) * spacing_of(count)


def wave_numbers(count):
    index = jnp.arange(count, dtype=jnp.int32)
    wrapped = jnp.where(index < count // 2, index, index - count)
    return wrapped.astype(jnp.float32) * (math.pi / VEL_RANGE)


def kernels(count):
    wave = wave_numbers(count)
    wave_y = wave[:, None, None]
    wave_x = wave[None, :, None]
    wave_z = wave[None, None, :]
    square = wave_y * wave_y + wave_x * wave_x + wave_z * wave_z
    first = 1.0 / (1.0 + square / 12.0)
    second = 3.0 * jnp.cos(0.9 * wave_x) / (1.0 + square / 10.0)
    damped = 1.0 + square / 9.0
    loss = 3.0 / (damped * damped)
    return (first, second, loss)


def dft_tables(count):
    index = jnp.arange(count, dtype=jnp.float32)
    angle = 2.0 * math.pi / count * index[:, None] * index[None, :]
    return (jnp.cos(angle), jnp.sin(angle))


def full_grid(count):
    index = jnp.arange(count * count * count, dtype=jnp.int32)
    velocity_y = speeds(index // (count * count), count)
    velocity_x = speeds(index // count % count, count)
    velocity_z = speeds(index % count, count)
    return (velocity_x, velocity_y, velocity_z)


def wall_tables(velocity_x, velocity_y, velocity_z):
    rest = jnp.exp(
        -(velocity_x * velocity_x + velocity_y * velocity_y + velocity_z * velocity_z) / 2.0
    )
    shifted = velocity_x - TOP_SPEED
    moving = jnp.exp(-(shifted * shifted + velocity_y * velocity_y + velocity_z * velocity_z) / 2.0)
    weights = jnp.stack(
        [
            jnp.maximum(-velocity_x, 0.0),
            jnp.maximum(velocity_x, 0.0),
            jnp.maximum(-velocity_y, 0.0),
            jnp.maximum(velocity_y, 0.0),
        ]
    )
    return (rest, moving, weights)


def wall_norms(count):
    velocity_x, velocity_y, velocity_z = full_grid(count)
    rest, moving, weights = wall_tables(velocity_x, velocity_y, velocity_z)
    return (
        jnp.sum(jnp.maximum(velocity_x, 0.0) * rest),
        jnp.sum(jnp.maximum(-velocity_x, 0.0) * rest),
        jnp.sum(jnp.maximum(velocity_y, 0.0) * rest),
        jnp.sum(jnp.maximum(-velocity_y, 0.0) * moving),
    )


def cell_masks(cell_type, groove_mask, height_count):
    total = cell_type.shape[0]
    solid = cell_type.astype(jnp.float32)
    height = jnp.arange(total, dtype=jnp.int32) % height_count
    left_solid = jnp.roll(solid, height_count)
    right_solid = jnp.roll(solid, -height_count)
    below_solid = jnp.where(height == 0, 1.0, jnp.roll(solid, 1))
    top_wall = jnp.where(height == height_count - 1, 1.0, 0.0 * solid)
    accommodation = jnp.repeat(jnp.where(groove_mask == 1, 1.0, ACC_LAND), height_count)
    return jnp.stack([left_solid, right_solid, below_solid, top_wall, accommodation, 1.0 - solid])


def advance(center, left, right, below, above, mirror, flux, masks, velocity, norms, step_size):
    velocity_x, velocity_y, rest, moving = velocity
    left_solid = masks[0][None, :]
    right_solid = masks[1][None, :]
    below_solid = masks[2][None, :]
    top_wall = masks[3][None, :]
    accommodation = masks[4][None, :]
    fluid = masks[5][None, :]
    left_ghost = (flux[0] / norms[0])[None, :] * rest
    right_ghost = (flux[1] / norms[1])[None, :] * rest
    below_ghost = (1.0 - accommodation) * mirror + accommodation * (flux[2] / norms[2])[
        None, :
    ] * rest
    above_ghost = (1.0 - ACC_TOP) * mirror + ACC_TOP * (flux[3] / norms[3])[None, :] * moving
    left_value = jnp.where(left_solid > 0.0, left_ghost, left)
    right_value = jnp.where(right_solid > 0.0, right_ghost, right)
    below_value = jnp.where(below_solid > 0.0, below_ghost, below)
    above_value = jnp.where(top_wall > 0.0, above_ghost, above)
    change = jnp.maximum(velocity_x, 0.0) * (center - left_value) + jnp.minimum(velocity_x, 0.0) * (
        right_value - center
    )
    change = (
        change
        + jnp.maximum(velocity_y, 0.0) * (center - below_value)
        + jnp.minimum(velocity_y, 0.0) * (above_value - center)
    )
    return (center - step_size * change) * fluid


def fourier_pass(real_part, imag_part, cosine, sine_table, form, forward):

    def apply(table, values):
        return jnp.einsum(form, table, values, precision=HIGHEST)

    if imag_part is None:
        return (apply(cosine, real_part), -apply(sine_table, real_part))
    if forward:
        return (
            apply(cosine, real_part) + apply(sine_table, imag_part),
            apply(cosine, imag_part) - apply(sine_table, real_part),
        )
    return (
        apply(cosine, real_part) - apply(sine_table, imag_part),
        apply(cosine, imag_part) + apply(sine_table, real_part),
    )


def collide(cube, tables, cosine, sine_table, rate):
    count = cube.shape[0]
    scale = 1.0 / (count * count * count)
    real_part, imag_part = fourier_pass(cube, None, cosine, sine_table, FORMS[0], True)
    real_part, imag_part = fourier_pass(real_part, imag_part, cosine, sine_table, FORMS[1], True)
    real_part, imag_part = fourier_pass(real_part, imag_part, cosine, sine_table, FORMS[2], True)

    def inverse(table):
        factor = table[..., None]
        first_real, first_imag = fourier_pass(
            real_part * factor, imag_part * factor, cosine, sine_table, FORMS[0], False
        )
        second_real, second_imag = fourier_pass(
            first_real, first_imag, cosine, sine_table, FORMS[1], False
        )
        last = jnp.einsum(FORMS[2], cosine, second_real, precision=HIGHEST) - jnp.einsum(
            FORMS[2], sine_table, second_imag, precision=HIGHEST
        )
        return last * scale

    gain = inverse(tables[0]) * inverse(tables[1])
    return cube + rate * (gain - cube * inverse(tables[2]))


def local(dist, cell_type, groove_mask):
    count = VN
    height_count = SY
    volume = count * count * count
    local_y, local_xz, total_cells = dist.shape
    masks = cell_masks(cell_type, groove_mask, height_count)
    norms = wall_norms(count)
    step_size = time_step(count)
    rate = step_size / KNUDSEN
    cosine, sine_table = dft_tables(count)
    tables = kernels(count)
    sub_index = lax.axis_index("sub")
    vel_index = lax.axis_index("vel")
    index_y = sub_index * local_y + jnp.arange(local_y, dtype=jnp.int32)
    index_xz = vel_index * local_xz + jnp.arange(local_xz, dtype=jnp.int32)
    block_shape = (local_y, local_xz)
    velocity_y = jnp.broadcast_to(speeds(index_y, count)[:, None], block_shape).reshape(-1)
    velocity_x = jnp.broadcast_to(speeds(index_xz // count, count)[None, :], block_shape).reshape(
        -1
    )
    velocity_z = jnp.broadcast_to(speeds(index_xz % count, count)[None, :], block_shape).reshape(-1)
    rest, moving, weights = wall_tables(velocity_x, velocity_y, velocity_z)
    velocity = (velocity_x[:, None], velocity_y[:, None], rest[:, None], moving[:, None])
    columns_total = total_cells // height_count
    depth = jnp.sum(cell_type.reshape(columns_total, height_count), axis=1)
    bottom_index = jnp.arange(columns_total, dtype=jnp.int32) * height_count + depth
    state = dist
    for iteration in range(STEPS):
        space = lax.all_to_all(
            lax.all_to_all(state, "vel", split_axis=2, concat_axis=1, tiled=True),
            "sub",
            split_axis=2,
            concat_axis=0,
            tiled=True,
        )
        cells = space.shape[2]
        post = collide(
            space.reshape(count, count, count, cells), tables, cosine, sine_table, rate
        ).reshape(volume, cells)
        back = lax.all_to_all(
            lax.all_to_all(
                post.reshape(count, count * count, 1, cells),
                "vel",
                split_axis=1,
                concat_axis=2,
                tiled=True,
            ),
            "sub",
            split_axis=0,
            concat_axis=3,
            tiled=True,
        )
        center = back.reshape(local_y * local_xz, total_cells)
        flux = lax.psum(jnp.dot(weights, center, precision=HIGHEST), ("vel", "sub"))
        shaped = center.reshape(local_y, local_xz, total_cells)
        bottom_rows = jnp.take(shaped, bottom_index, axis=2)
        top_rows = shaped[:, :, height_count - 1 :: height_count]
        outgoing = jnp.where(sub_index == 0, bottom_rows, top_rows)
        incoming = swapped(outgoing, "sub", 0)
        mirror = jnp.repeat(incoming[::-1], height_count, axis=2).reshape(
            local_y * local_xz, total_cells
        )
        result = advance(
            center,
            jnp.roll(center, height_count, 1),
            jnp.roll(center, -height_count, 1),
            jnp.roll(center, 1, 1),
            jnp.roll(center, -1, 1),
            mirror,
            flux,
            masks,
            velocity,
            norms,
            step_size,
        )
        state = result.reshape(local_y, local_xz, total_cells)
    return state


def solution(mesh):
    return jax.shard_map(
        local,
        mesh=mesh,
        in_specs=(P("sub", "vel", "groups"), P("groups"), P("groups")),
        out_specs=P("sub", "vel", "groups"),
        check_vma=False,
    )
```

profile of v0, /device:TPU:1, one launch (start us, length us, event | category | flops | bytes accessed | tf_op | source)
XLA Modules:
  0.0 529.2 jit_solution(7535001363961206787)
XLA Ops:
  3.6 6.4 %all-to-all-start = ((f32[8,1,16384]{2,1,0:T(1,128)}), f32[8,1,16384]{2,1,0:T(1,128)S(1)}, u32[]{:S(2)}, u32[]{:S(2)}) async-start(f32[8,1,16384]{2,1,0:T(1,128)} %reshape.613), calls=%async_computation | async-start | bytes 1048576 | tf_op jit(solution)/shard_map/all_to_all | solution.py:213
  19.5 3.9 all-to-all-done
  27.4 5.8 %all_to_all.132 = f32[8,256,64]{1,0,2:T(8,128)S(1)} all-to-all(f32[8,256,64]{1,0,2:T(8,128)S(1)} %copy.780), channel_id=1, replica_groups=mesh['groups'=2,'vel'=8,'sub'=2] {'sub'}, dimensions={2} | all-to-all | bytes 1048576 | tf_op jit(solution)/shard_map/all_to_all | solution.py:212
  38.6 3.3 fusion.158
  45.2 3.5 subtract_bitcast_fusion.7
  53.7 3.4 add_bitcast_fusion.7
  59.8 3.4 multiply_bitcast_fusion.10
  69.0 3.4 fusion.179
  72.4 3.4 fusion.134
  88.0 3.4 fusion.102
  91.4 3.5 fusion.104
  103.7 3.8 fusion.118
  113.7 3.4 subtract_bitcast_fusion.6
  117.1 3.5 add_bitcast_fusion.6
  128.5 3.6 subtract_bitcast_fusion.4
  132.2 3.4 add_bitcast_fusion.4
  140.6 3.4 fusion.186
  144.0 3.4 subtract_bitcast_fusion.5
  147.4 3.3 add_bitcast_fusion.5
  155.9 8.6 %fusion.5 = f32[16,16,16,32]{3,0,2,1:T(8,128)} fusion(f32[16,16,16,32]{3,0,2,1:T(8,128)S(1)} %bitcast.348, f32[16,16,32,16]{2,3,1,0:T(8,128)S(1)} %fusion.23, f32[16,16,32,16]{2,3,1,0:T(8,128)S(1)} %fusion.25, f32[16,16,32,16]{2,3,1,0:T(8,128)S(1)} %fusion.29, f32[16,16,32,16]{2,3,1,0:T(8,128)S(1)} %fusion.31, f32[16,16,32,16]{2,3,1,0:T(8,128)S(1)} %fusion.34, ...), kind=kLoop, calls=%fused_computation.9 | loop fusion | flops 1441792 | bytes 4194304 | tf_op jit(solution)/shard_map/add | solution.py:181
  167.6 3.7 all-to-all-start.2
  177.3 7.6 %all-to-all-done.2 = f32[8,1,16384]{2,1,0:T(1,128)S(1)} async-done(((f32[8,1,16384]{2,1,0:T(1,128)}), f32[8,1,16384]{2,1,0:T(1,128)S(1)}, u32[]{:S(2)}, u32[]{:S(2)}) %all-to-all-start.2) | async-done | bytes 524320 | tf_op jit(solution)/shard_map/all_to_all | solution.py:224
  192.0 5.5 %all_to_all.133 = f32[2,1,65536]{2,1,0:T(1,128)S(1)} all-to-all(f32[2,1,65536]{2,1,0:T(1,128)S(1)} %reshape.617), channel_id=1, replica_groups=mesh['groups'=2,'vel'=8,'sub'=2] {'sub'}, dimensions={0} | all-to-all | bytes 1048576 | tf_op jit(solution)/shard_map/all_to_all | solution.py:223
  217.7 30.7 %psum.14 = f32[4,512]{1,0:T(4,128)} all-reduce(f32[4,512]{1,0:T(4,128)} %fusion.572), channel_id=1, replica_groups=mesh['groups'=2,'vel'=8,'sub'=2] {'vel','sub'}, use_global_device_ids=true, to_apply=%region_0.1 | all-reduce | flops 2048 | bytes 16384 | tf_op jit(solution)/shard_map/psum | solution.py:237
  254.5 4.1 slice_divide_fusion.5
  269.2 3.3 fusion.253
  275.2 16.8 %all_to_all.134 = f32[8,1,16384]{2,1,0:T(1,128)S(1)} all-to-all(f32[8,1,16384]{2,1,0:T(1,128)S(1)} %reshape.619), channel_id=1, replica_groups=mesh['groups'=2,'vel'=8,'sub'=2] {'vel'}, dimensions={0} | all-to-all | bytes 1048576 | tf_op jit(solution)/shard_map/all_to_all | solution.py:213
  295.6 4.9 all_to_all.135
  305.8 3.4 fusion.94
  309.1 3.3 fusion.96
  312.4 3.5 subtract_bitcast_fusion.3
  320.9 3.4 add_bitcast_fusion.3
  327.3 3.4 multiply_bitcast_fusion.4
  339.6 3.4 fusion.70
  355.2 3.4 fusion.38
  358.6 3.7 fusion.40
  371.1 3.5 fusion.54
  374.6 3.3 fusion.56
  380.9 3.3 subtract_bitcast_fusion.2
  384.3 3.5 add_bitcast_fusion.2
  395.8 3.8 subtract_bitcast_fusion
  399.6 3.4 add_bitcast_fusion
  411.2 3.4 subtract_bitcast_fusion.1
  414.6 3.3 add_bitcast_fusion.1
  423.1 8.6 %fusion.2 = f32[16,16,16,32]{3,0,2,1:T(8,128)} fusion(f32[16,16,16,32]{3,0,2,1:T(8,128)S(1)} %bitcast.345, f32[16,16,32,16]{2,3,1,0:T(8,128)S(1)} %fusion.7, f32[16,16,32,16]{2,3,1,0:T(8,128)S(1)} %fusion.9, f32[16,16,32,16]{2,3,1,0:T(8,128)S(1)} %fusion.13, f32[16,16,32,16]{2,3,1,0:T(8,128)S(1)} %fusion.15, f32[16,16,32,16]{2,3,1,0:T(8,128)S(1)} %fusion.18, ...), kind=kLoop, calls=%fused_computation.5 | loop fusion | flops 1441792 | bytes 4194304 | tf_op jit(solution)/shard_map/add | solution.py:181
  434.1 17.2 %all_to_all.136 = f32[8,1,16384]{2,1,0:T(1,128)S(1)} all-to-all(f32[8,1,16384]{2,1,0:T(1,128)S(1)} %reshape.621), channel_id=1, replica_groups=mesh['groups'=2,'vel'=8,'sub'=2] {'vel'}, dimensions={0} | all-to-all | bytes 1048576 | tf_op jit(solution)/shard_map/all_to_all | solution.py:224
  458.5 5.5 %all_to_all.137 = f32[2,1,65536]{2,1,0:T(1,128)S(1)} all-to-all(f32[2,1,65536]{2,1,0:T(1,128)S(1)} %reshape.623), channel_id=1, replica_groups=mesh['groups'=2,'vel'=8,'sub'=2] {'sub'}, dimensions={0} | all-to-all | bytes 1048576 | tf_op jit(solution)/shard_map/all_to_all | solution.py:223
  481.7 29.9 %psum.15 = f32[4,512]{1,0:T(4,128)S(1)} all-reduce(f32[4,512]{1,0:T(4,128)S(1)} %fusion.571), channel_id=1, replica_groups=mesh['groups'=2,'vel'=8,'sub'=2] {'vel','sub'}, use_global_device_ids=true, to_apply=%region_6.8 | all-reduce | flops 2048 | bytes 16384 | tf_op jit(solution)/shard_map/psum | solution.py:237
  (243 shorter events, 255.4 us)
Async XLA Ops:
  1.8 11.1 %copy-start.33 = (s32[32]{0:T(128)S(1)}, s32[32]{0:T(128)}, u32[]{:S(2)}) copy-start(s32[32]{0:T(128)} %param.7) | copy-start | bytes 388
  1.8 11.1 %copy-start.12 = (s32[512]{0:T(512)S(1)}, s32[512]{0:T(512)}, u32[]{:S(2)}) copy-start(s32[512]{0:T(512)} %param.6) | copy-start | bytes 6148
  3.6 19.8 %all-to-all-start = ((f32[8,1,16384]{2,1,0:T(1,128)}), f32[8,1,16384]{2,1,0:T(1,128)S(1)}, u32[]{:S(2)}, u32[]{:S(2)}) async-start(f32[8,1,16384]{2,1,0:T(1,128)} %reshape.613), calls=%async_computation | async-start | bytes 1048576 | tf_op jit(solution)/shard_map/all_to_all | solution.py:213
  10.5 8.9 %copy-start.23 = (f32[8]{0:T(128)}, f32[8]{0:T(128)S(1)}, u32[]{:S(2)}) copy-start(f32[8]{0:T(128)S(1)} %get-tuple-element.71) | copy-start | bytes 100
  12.9 6.5 %copy-start.24 = (f32[32]{0:T(128)}, f32[32]{0:T(128)S(1)}, u32[]{:S(2)}) copy-start(f32[32]{0:T(128)S(1)} %get-tuple-element.67) | copy-start | bytes 388
  17.3 251.8 %copy-start.13 = (f32[512]{0:T(512)}, f32[512]{0:T(512)S(1)}, u32[]{:S(2)}) copy-start(f32[512]{0:T(512)S(1)} %sub.287) | copy-start | bytes 6148
  164.4 9.6 %copy-start.21 = (f32[496]{0:T(512)S(1)}, f32[496]{0:T(512)}, u32[]{:S(2)}) copy-start(f32[496]{0:T(512)} %get-tuple-element.55) | copy-start | bytes 5956
  164.4 9.6 %copy-start.22 = (f32[496]{0:T(512)S(1)}, f32[496]{0:T(512)}, u32[]{:S(2)}) copy-start(f32[496]{0:T(512)} %get-tuple-element.56) | copy-start | bytes 5956
  164.4 9.6 %copy-start.26 = (f32[16]{0:T(128)S(1)}, f32[16]{0:T(128)}, u32[]{:S(2)}) copy-start(f32[16]{0:T(128)} %get-tuple-element.53) | copy-start | bytes 196
  164.5 9.6 %copy-start.27 = (f32[16]{0:T(128)S(1)}, f32[16]{0:T(128)}, u32[]{:S(2)}) copy-start(f32[16]{0:T(128)} %get-tuple-element.54) | copy-start | bytes 196
  164.5 10.3 %copy-start.32 = (s32[32]{0:T(128)S(1)}, s32[32]{0:T(128)}, u32[]{:S(2)}) copy-start(s32[32]{0:T(128)} %get-tuple-element.11) | copy-start | bytes 388
  164.5 12.7 %copy-start.28 = (f32[8]{0:T(128)S(1)}, f32[8]{0:T(128)}, u32[]{:S(2)}) copy-start(f32[8]{0:T(128)} %get-tuple-element.72) | copy-start | bytes 100
  164.5 12.7 %copy-start.29 = (f32[32]{0:T(128)S(1)}, f32[32]{0:T(128)}, u32[]{:S(2)}) copy-start(f32[32]{0:T(128)} %get-tuple-element.63) | copy-start | bytes 388
  164.5 12.7 %copy-start.30 = (f32[32]{0:T(128)S(1)}, f32[32]{0:T(128)}, u32[]{:S(2)}) copy-start(f32[32]{0:T(128)} %get-tuple-element.64) | copy-start | bytes 388
  164.5 12.7 %copy-start.31 = (f32[32]{0:T(128)S(1)}, f32[32]{0:T(128)}, u32[]{:S(2)}) copy-start(f32[32]{0:T(128)} %get-tuple-element.68) | copy-start | bytes 388
  167.6 17.3 %all-to-all-start.2 = ((f32[8,1,16384]{2,1,0:T(1,128)}), f32[8,1,16384]{2,1,0:T(1,128)S(1)}, u32[]{:S(2)}, u32[]{:S(2)}) async-start(f32[8,1,16384]{2,1,0:T(1,128)} %reshape.615), calls=%async_computation.2 | async-start | bytes 1048576 | tf_op jit(solution)/shard_map/all_to_all | solution.py:224
  177.3 91.9 %copy-start.8 = (f32[8,32]{1,0:T(8,128)}, f32[8,32]{1,0:T(8,128)S(1)}, u32[]{:S(2)}) copy-start(f32[8,32]{1,0:T(8,128)S(1)} %get-tuple-element.57) | copy-start | bytes 3076
  177.3 91.9 %copy-start.10 = (f32[8,32]{1,0:T(8,128)}, f32[8,32]{1,0:T(8,128)S(1)}, u32[]{:S(2)}) copy-start(f32[8,32]{1,0:T(8,128)S(1)} %get-tuple-element.58) | copy-start | bytes 3076
  207.8 2.7 copy-start.1
  249.8 15.5 %copy-start.7 = (f32[256,496]{0,1:T(8,128)S(1)}, f32[256,496]{0,1:T(8,128)}, u32[]{:S(2)}) copy-start(f32[256,496]{0,1:T(8,128)} %get-tuple-element.33) | copy-start | bytes 1523716
  249.8 16.5 %copy-start.5 = (f32[256,511]{0,1:T(8,128)S(1)}, f32[256,511]{0,1:T(8,128)}, u32[]{:S(2)}) copy-start(f32[256,511]{0,1:T(8,128)} %get-tuple-element.30) | copy-start | bytes 1569796
  250.9 16.4 %copy-start.4 = (f32[256,511]{0,1:T(8,128)S(1)}, f32[256,511]{0,1:T(8,128)}, u32[]{:S(2)}) copy-start(f32[256,511]{0,1:T(8,128)} %get-tuple-element.31) | copy-start | bytes 1569796
  251.9 16.4 %collective-permute-start = (f32[8,32,32]{2,1,0:T(8,128)S(1)}, f32[8,32,32]{2,1,0:T(8,128)S(1)}, u32[]{:S(2)}, u32[]{:S(2)}) collective-permute-start(f32[8,32,32]{2,1,0:T(8,128)S(1)} %bitcast_select_fusion.1), channel_id=1, source_target_pairs={{0,1},{1,0},{2,3},{3,2},{4,5},{5,4},{6,7},{7,6},{8,9},{9,8},{10,11... | collective-permute-start | bytes 98312 | tf_op jit(solution)/shard_map/ppermute | solution.py:25
  472.1 2.2 copy-start.17
  472.1 2.2 copy-start.18
  472.1 2.2 copy-start.19
  472.1 2.2 copy-start.20
  474.8 2.1 copy-start
  479.6 32.0 %copy-start.16 = (f32[1,512]{1,0:T(1,128)S(1)}, f32[1,512]{1,0:T(1,128)}, u32[]{:S(2)}) copy-start(f32[1,512]{1,0:T(1,128)} %stack_reshape.3) | copy-start | bytes 6148
  479.6 36.1 %copy-start.25 = (pred[32]{0:T(512)(128)(4,1)S(1)}, pred[32]{0:T(512)(128)(4,1)}, u32[]{:S(2)}) copy-start(pred[32]{0:T(512)(128)(4,1)} %get-tuple-element.10) | copy-start | bytes 100
  515.5 6.3 %copy-start.6 = (f32[256,496]{0,1:T(8,128)S(1)}, f32[256,496]{0,1:T(8,128)}, u32[]{:S(2)}) copy-start(f32[256,496]{0,1:T(8,128)} %get-tuple-element.27) | copy-start | bytes 1523716
  515.5 7.3 %copy-start.3 = (f32[256,511]{0,1:T(8,128)S(1)}, f32[256,511]{0,1:T(8,128)}, u32[]{:S(2)}) copy-start(f32[256,511]{0,1:T(8,128)} %get-tuple-element.24) | copy-start | bytes 1569796
  515.7 8.2 %copy-start.2 = (f32[256,511]{0,1:T(8,128)S(1)}, f32[256,511]{0,1:T(8,128)}, u32[]{:S(2)}) copy-start(f32[256,511]{0,1:T(8,128)} %get-tuple-element.25) | copy-start | bytes 1569796
  515.7 9.2 %collective-permute-start.1 = (f32[8,32,32]{2,1,0:T(8,128)S(1)}, f32[8,32,32]{2,1,0:T(8,128)S(1)}, u32[]{:S(2)}, u32[]{:S(2)}) collective-permute-start(f32[8,32,32]{2,1,0:T(8,128)S(1)} %bitcast_select_fusion), channel_id=1, source_target_pairs={{0,1},{1,0},{2,3},{3,2},{4,5},{5,4},{6,7},{7,6},{8,9},{9,8},{10,11... | collective-permute-start | bytes 98312 | tf_op jit(solution)/shard_map/ppermute | solution.py:25
  525.0 0.8 copy-start.9
  525.0 0.8 copy-start.11
  525.1 0.8 copy-start.14
  525.1 0.8 copy-start.15
where the time goes:
time: 535 us; the launch traced here: 529 us
  matrix products  244 us (46%)
  blocking collectives  116 us (22%)
  local copies, waits for them, and re-layouts  86.8 us (16%)
  other arithmetic  53.3 us (10%)
  starting transfers between devices  15.5 us (3%)
  waiting for transfers between devices  11.5 us (2%)
    dot_general x68, matrix products, apply(): return jnp.einsum(form, table, values, precision=HIGHEST)  212 us
    psum x2, blocking collectives, local(): flux = lax.psum(jnp.dot(weights, center, precision=HIGHEST), ('vel', 'sub'))  60.6 us
    unnamed x83, local copies, waits for them, and re-layouts  20 us
    all_to_all x1, blocking collectives, local(): lax.all_to_all(post.reshape(count, count * count, 1, cells), 'vel', split...  17.2 us
    add x2, other arithmetic, collide(): return cube + rate * (gain - cube * inverse(tables[2]))  17.1 us
    all_to_all x1, blocking collectives, local(): lax.all_to_all(state, 'vel', split_axis=2, concat_axis=1, tiled=True)  16.8 us
    dot_general x6, matrix products, inverse(): jnp.einsum(FORMS[2], cosine, second_real, precision=HIGHEST)  15.3 us
    dot_general x6, matrix products, inverse(): jnp.einsum(FORMS[2], sine_table, second_imag, precision=HIGHEST)  15 us
  transfers between devices with their start and end apart: 4, of which 2 were waited for; matrix products, arithmetic and copies ran while one was open for 7% of the time, Pallas kernels for 0%

commit v1 on v0

v1 whole, which is shorter than its diff:
```python
import functools
import math

import jax
import jax.numpy as jnp
import numpy as np
from jax import lax
from jax.experimental import pallas as pl
from jax.experimental.pallas import tpu as pltpu
from jax.sharding import PartitionSpec as P

VN = 16
SY = 16
STEPS = 2

VEL_RANGE = 5.0
TOP_SPEED = 1.0
ACC_LAND = 0.4
ACC_TOP = 0.7
KNUDSEN = 1.0
HALF = VN // 2
PLANE = VN * VN
LANES = 128
CHUNK = 32
MESH = pl.DeviceIdType.MESH
F32 = jnp.float32
BF16 = jnp.bfloat16


def real_basis():
    place = np.arange(VN) - (VN - 1) / 2.0
    modes = np.concatenate([np.arange(HALF), np.arange(1, HALF + 1)])
    rows = []
    for index, mode in enumerate(modes):
        angle = 2.0 * math.pi * mode * place / VN
        row = np.cos(angle) if index < HALF else np.sin(angle)
        rows.append(row / np.sqrt(np.sum(row * row)))
    return modes, np.stack(rows)


def halves(table):
    high = table.astype(np.float32).astype(jnp.bfloat16)
    low = (table - high.astype(np.float64)).astype(jnp.bfloat16)
    return high, low


def left_table(table):
    high, low = halves(table)
    return np.concatenate([high, high, low], axis=1)


def right_table(table):
    high, low = halves(table)
    return np.concatenate([high, high, low], axis=0)


@functools.cache
def constants():
    modes, basis = real_basis()
    step = 2.0 * VEL_RANGE / VN
    plane = np.kron(basis, basis)
    same = np.eye(CHUNK)
    forward = left_table(plane)
    inverse = left_table(plane.T)
    even = np.kron(basis[:HALF, :HALF].T, same)
    odd = np.kron(basis[HALF:, :HALF].T, same)
    height = np.stack([right_table(t) for t in (even, odd, even.T, odd.T)])
    wave = modes * (math.pi / VEL_RANGE)
    along_y = wave[:, None, None]
    along_x = wave[None, :, None]
    along_z = wave[None, None, :]
    square = along_y**2 + along_x**2 + along_z**2
    first = 1.0 / (1.0 + square / 12.0)
    second = 3.0 * np.cos(0.9 * along_x) / (1.0 + square / 10.0)
    loss = 3.0 / (1.0 + square / 9.0) ** 2
    tables = []
    for table in (first, second, loss):
        table = table.reshape(2, HALF, PLANE).transpose(0, 2, 1)
        tables.append(np.repeat(table, CHUNK, axis=2))
    tables = np.stack(tables).astype(np.float32)

    speed = (np.arange(VN) - (VN - 1) / 2.0) * step
    dt = 0.8 / ((VN - 1) * step)
    gauss = np.exp(-speed * speed / 2.0)
    moving = np.exp(-((speed - TOP_SPEED) ** 2) / 2.0)
    speed_x = np.repeat(speed, VN)
    rows = np.stack([np.abs(speed_x), np.kron(gauss, gauss), np.kron(moving, gauss)])
    rows = np.broadcast_to(rows[:, :, None], (3, PLANE, LANES)).astype(np.float32)
    lanes = np.zeros((8, LANES))
    for part in range(2):
        lanes[part] = np.repeat(np.abs(speed[4 * part : 4 * part + 4]), CHUNK)
        lanes[2 + part] = np.repeat(gauss[4 * part : 4 * part + 4], CHUNK)
    up = np.sum(np.maximum(speed, 0.0) * gauss)
    total = np.sum(gauss)
    norms = (
        up * total * total,
        up * total * total,
        up * total * total,
        up * np.sum(moving) * total,
    )
    return forward, inverse, height, tables, rows, lanes.astype(np.float32), dt, norms


def roll(value, shift):
    return pltpu.roll(value, shift % LANES, 1)


def chunk_transpose(parts, low_pair, even_chunk):
    a0, a1, a2, a3 = parts
    b0 = jnp.where(low_pair, a0, roll(a2, 64))
    b2 = jnp.where(low_pair, roll(a0, 64), a2)
    b1 = jnp.where(low_pair, a1, roll(a3, 64))
    b3 = jnp.where(low_pair, roll(a1, 64), a3)
    return (
        jnp.where(even_chunk, b0, roll(b1, 32)),
        jnp.where(even_chunk, roll(b0, -32), b1),
        jnp.where(even_chunk, b2, roll(b3, 32)),
        jnp.where(even_chunk, roll(b2, -32), b3),
    )


def split(value):
    high = value.astype(BF16)
    low = (value - high.astype(F32)).astype(BF16)
    return high, low


def kernel(
    vel_count, dt, norms,
    cell_ref, groove_ref, dist_ref, forward_hbm, inverse_hbm, height_hbm, tables_hbm, rows_hbm,
    lanes_ref, out_ref,
    stage, back, grid, post, gains, halo_out, halo_in, forward, inverse, height, tables, rows,
    table_sem, own_sem, send_sem, recv_sem, halo_send, halo_recv, back_send, back_recv,
):
    devices = 2 * vel_count
    depth = dist_ref.shape[1]
    group = lax.axis_index("groups")
    vel = lax.axis_index("vel")
    sub = lax.axis_index("sub")
    ring = vel // 2 + (vel % 2) * (vel_count - 1 - 2 * (vel // 2))
    me = 2 * ring + sub

    def place_of(position):
        index = position // 2
        far = index // (vel_count // 2)
        return 2 * index + far * (2 * (vel_count - 1 - index) + 1 - 2 * index), position % 2

    def device_of(position):
        v, s = place_of(position)
        return (group, v, s)

    loads = [
        pltpu.make_async_copy(source, target, table_sem.at[index])
        for index, (source, target) in enumerate(
            (
                (forward_hbm, forward),
                (inverse_hbm, inverse),
                (height_hbm, height),
                (tables_hbm, tables),
                (rows_hbm, rows),
            )
        )
    ]
    for load in loads:
        load.start()

    barrier = pltpu.get_barrier_semaphore()

    @pl.loop(1, devices)
    def _(offset):
        pl.semaphore_signal(
            barrier, inc=1, device_id=device_of((me + offset) % devices), device_id_type=MESH
        )

    pl.semaphore_wait(barrier, devices - 1)

    lane = lax.broadcasted_iota(jnp.int32, (1, LANES), 1)
    low_pair = lane < 64
    even_chunk = lane % 64 < 32
    first_column = lane % CHUNK < SY
    level = lane % SY

    def outward(position):
        return pltpu.make_async_remote_copy(
            src_ref=stage.at[position],
            dst_ref=grid.at[pl.ds(2 * sub, 2), pl.ds(vel * depth, depth), :],
            send_sem=send_sem.at[position],
            recv_sem=recv_sem.at[me],
            device_id=device_of(position),
            device_id_type=MESH,
        )

    @pl.loop(0, devices // 4)
    def _(turn):
        block = (turn + me // 4) % (devices // 4)
        start = pl.multiple_of(block * LANES, LANES)
        for part in range(2):
            pieces = []
            for index in range(4):
                m = 4 * part + index
                y = m + sub * (HALF - 1 - 2 * m)
                pieces.append(dist_ref[y, :, pl.ds(start, LANES)])
            for index, piece in enumerate(chunk_transpose(pieces, low_pair, even_chunk)):
                stage[4 * block + index, part] = piece
        for index in range(4):
            position = 4 * block + index

            @pl.when(position != me)
            def _():
                outward(position).start()

    own = pltpu.make_async_copy(
        stage.at[me], grid.at[pl.ds(2 * sub, 2), pl.ds(vel * depth, depth), :], own_sem.at[0]
    )
    own.start()

    cells = CHUNK * devices

    def solid_count(column):
        count = jnp.int32(0)
        for index in range(SY):
            count = count + cell_ref[column * SY + index]
        return count

    columns = cells // SY
    count_first = solid_count(2 * me)
    count_second = solid_count(2 * me + 1)
    count_left = solid_count((2 * me + columns - 1) % columns)
    count_right = solid_count((2 * me + 2) % columns)
    count = jnp.where(first_column, count_first, count_second)
    left_solid = level < jnp.where(first_column, count_left, count_first)
    right_solid = level < jnp.where(first_column, count_second, count_right)
    below_solid = level <= count
    top_wall = level == SY - 1
    fluid = jnp.where(level < count, 0.0, 1.0)
    groove = jnp.where(first_column, groove_ref[2 * me], groove_ref[2 * me + 1])
    accommodation = jnp.where(groove == 1, 1.0, ACC_LAND)

    for load in loads:
        load.wait()
    own.wait()

    @pl.loop(1, devices)
    def _(offset):
        source = (me + devices - offset) % devices
        v, s = place_of(source)
        pltpu.make_async_remote_copy(
            src_ref=stage.at[source],
            dst_ref=grid.at[pl.ds(2 * s, 2), pl.ds(v * depth, depth), :],
            send_sem=send_sem.at[source],
            recv_sem=recv_sem.at[source],
            device_id=device_of(source),
            device_id_type=MESH,
        ).wait_recv()

    rate = dt / KNUDSEN
    right_device = device_of((me + 1) % devices)
    left_device = device_of((me + devices - 1) % devices)

    def by_height(value, index):
        high, low = split(value)
        return jnp.dot(
            jnp.concatenate([high, low, high], axis=1), height[index], preferred_element_type=F32
        )

    def by_plane(table, value):
        high, low = split(value)
        return jnp.dot(
            table[...], jnp.concatenate([high, low, high], axis=0), preferred_element_type=F32
        )

    @pl.loop(0, STEPS)
    def _(step):
        for parity in range(2):
            if parity == 0:
                folded = [grid[0] + grid[2], grid[1] + grid[3]]
            else:
                folded = [grid[0] - grid[2], grid[1] - grid[3]]
            spectrum = by_plane(forward, by_height(jnp.concatenate(folded, axis=1), parity))
            for index in range(3):
                gains[index, parity] = by_height(
                    by_plane(inverse, spectrum * tables[index, parity]), 2 + parity
                )

        def collided(q, low, high):
            part = q % 2
            lanes = slice(LANES * part, LANES * part + LANES)
            found = []
            for index in range(3):
                even = gains[index, 0, low:high, lanes]
                odd = gains[index, 1, low:high, lanes]
                found.append(even + odd if q < 2 else even - odd)
            value = grid[q, low:high]
            return value + rate * (found[0] * found[1] - value * found[2])

        flux_x = [jnp.zeros((1, LANES), F32), jnp.zeros((1, LANES), F32)]
        flux_y = [jnp.zeros((1, LANES), F32), jnp.zeros((1, LANES), F32)]
        copies = []
        for side in range(2):
            low, high = side * (PLANE // 2), (side + 1) * (PLANE // 2)
            for pair in range(2):
                values = []
                for part in range(2):
                    q = 2 * pair + part
                    value = collided(q, low, high)
                    post[q, low:high] = value
                    values.append(value)
                    flux_x[side] = flux_x[side] + jnp.sum(
                        value * rows[0, low:high], axis=0, keepdims=True
                    )
                    flux_y[pair] = flux_y[pair] + lanes_ref[part : part + 1] * jnp.sum(
                        value, axis=0, keepdims=True
                    )
                if side == 0:
                    packed = jnp.where(first_column, values[1], roll(values[0], SY))
                else:
                    packed = jnp.where(first_column, roll(values[0], -SY), values[1])
                halo_out[2 * step + side, pair] = packed
            copy = pltpu.make_async_remote_copy(
                src_ref=halo_out.at[2 * step + side],
                dst_ref=halo_in.at[2 * step + side],
                send_sem=halo_send.at[2 * step + side],
                recv_sem=halo_recv.at[2 * step + side],
                device_id=left_device if side == 0 else right_device,
                device_id_type=MESH,
            )
            copy.start()
            copies.append(copy)

        def over_chunks(value):
            value = value + roll(value, 64)
            return value + roll(value, 32)

        flux = [over_chunks(f) for f in flux_x + flux_y]
        for side in range(2):
            low, high = side * (PLANE // 2), (side + 1) * (PLANE // 2)
            copies[side].wait()
            for pair in range(2):
                packed = halo_in[2 * step + side, pair]
                for part in range(2):
                    q = 2 * pair + part
                    center = post[q, low:high]
                    mirror = post[2 * (1 - pair) + part, low:high]
                    gauss_y = lanes_ref[2 + part : 3 + part]
                    if side == 0:
                        edge = packed if part == 0 else roll(packed, SY)
                        across = jnp.where(first_column, roll(center, -SY), edge)
                        solid = right_solid
                        scale = flux[1] / norms[1]
                    else:
                        edge = packed if part == 0 else roll(packed, -SY)
                        across = jnp.where(first_column, edge, roll(center, SY))
                        solid = left_solid
                        scale = flux[0] / norms[0]
                    rest = rows[1, low:high]
                    across = jnp.where(solid, rest * (scale * gauss_y), across)
                    if pair == 0:
                        ghost = (1.0 - ACC_TOP) * mirror + rows[2, low:high] * (
                            flux[3] * (gauss_y * (ACC_TOP / norms[3]))
                        )
                        along = jnp.where(top_wall, ghost, roll(center, -1))
                    else:
                        ghost = (1.0 - accommodation) * mirror + rest * (
                            accommodation * flux[2] * (gauss_y / norms[2])
                        )
                        along = jnp.where(below_solid, ghost, roll(center, 1))
                    change = rows[0, low:high] * (center - across) + lanes_ref[
                        part : part + 1
                    ] * (center - along)
                    grid[q, low:high] = (center - dt * change) * fluid

    def homeward(position):
        v, s = place_of(position)
        return pltpu.make_async_remote_copy(
            src_ref=grid.at[pl.ds(2 * s, 2), pl.ds(v * depth, depth), :],
            dst_ref=back.at[me],
            send_sem=back_send.at[position],
            recv_sem=back_recv.at[me],
            device_id=device_of(position),
            device_id_type=MESH,
        )

    @pl.loop(1, devices)
    def _(offset):
        homeward((me + offset) % devices).start()

    own_back = pltpu.make_async_copy(
        grid.at[pl.ds(2 * sub, 2), pl.ds(vel * depth, depth), :], back.at[me], own_sem.at[1]
    )
    own_back.start()

    @pl.loop(1, devices)
    def _(offset):
        outward((me + offset) % devices).wait_send()

    own_back.wait()

    @pl.loop(1, devices)
    def _(offset):
        source = (me + devices - offset) % devices
        pltpu.make_async_remote_copy(
            src_ref=stage.at[source],
            dst_ref=back.at[source],
            send_sem=back_send.at[source],
            recv_sem=back_recv.at[source],
            device_id=device_of(source),
            device_id_type=MESH,
        ).wait_recv()

    @pl.loop(0, devices // 4)
    def _(block):
        start = pl.multiple_of(block * LANES, LANES)
        for part in range(2):
            pieces = [back[4 * block + index, part] for index in range(4)]
            for index, piece in enumerate(chunk_transpose(pieces, low_pair, even_chunk)):
                m = 4 * part + index
                y = m + sub * (HALF - 1 - 2 * m)
                out_ref[y, :, pl.ds(start, LANES)] = piece

    @pl.loop(1, devices)
    def _(offset):
        homeward((me + offset) % devices).wait_send()


def solution(mesh):
    vel_count = mesh.shape["vel"]
    devices = 2 * vel_count
    forward, inverse, height, tables, rows, lanes, dt, norms = constants()
    depth = PLANE // vel_count

    def local(dist, cell_type, groove_mask):
        hbm = pl.BlockSpec(memory_space=pl.ANY)
        vmem = pl.BlockSpec(memory_space=pltpu.VMEM)
        smem = pl.BlockSpec(memory_space=pltpu.SMEM)
        dma = pltpu.SemaphoreType.DMA
        piece = (2, depth, LANES)
        return pl.pallas_call(
            functools.partial(kernel, vel_count, dt, norms),
            out_shape=jax.ShapeDtypeStruct(dist.shape, F32),
            in_specs=[smem, smem, vmem, hbm, hbm, hbm, hbm, hbm, vmem],
            out_specs=vmem,
            scratch_shapes=[
                pltpu.VMEM((devices,) + piece, F32),
                pltpu.VMEM((devices,) + piece, F32),
                pltpu.VMEM((4, PLANE, LANES), F32),
                pltpu.VMEM((4, PLANE, LANES), F32),
                pltpu.VMEM((3, 2, PLANE, PLANE), F32),
                pltpu.VMEM((2 * STEPS, 2, PLANE // 2, LANES), F32),
                pltpu.VMEM((2 * STEPS, 2, PLANE // 2, LANES), F32),
                pltpu.VMEM(forward.shape, BF16),
                pltpu.VMEM(inverse.shape, BF16),
                pltpu.VMEM(height.shape, BF16),
                pltpu.VMEM(tables.shape, F32),
                pltpu.VMEM(rows.shape, F32),
                dma((5,)),
                dma((2,)),
                dma((devices,)),
                dma((devices,)),
                dma((2 * STEPS,)),
                dma((2 * STEPS,)),
                dma((devices,)),
                dma((devices,)),
            ],
            compiler_params=pltpu.CompilerParams(
                collective_id=0, has_side_effects=True, vmem_limit_bytes=40 * 1024 * 1024
            ),
        )(
            cell_type, groove_mask, dist,
            jnp.asarray(forward), jnp.asarray(inverse), jnp.asarray(height),
            jnp.asarray(tables), jnp.asarray(rows), jnp.asarray(lanes),
        )

    return jax.shard_map(
        local,
        mesh=mesh,
        in_specs=(P("sub", "vel", "groups"), P("groups"), P("groups")),
        out_specs=P("sub", "vel", "groups"),
        check_vma=False,
    )
```

time: 535 us -> 59.3 us (0.11); the launches traced: 529 us -> 58.9 us
  matrix products: 244 us -> 0 us
  blocking collectives: 116 us -> 0 us
  local copies, waits for them, and re-layouts: 86.8 us -> 9.66 us
  other arithmetic: 53.3 us -> 0 us
  Pallas kernels: 0 us -> 49.2 us
  starting transfers between devices: 15.5 us -> 0 us
  waiting for transfers between devices: 11.5 us -> 0 us
    dot_general x82 -> x0, matrix products: 244 us -> none  [the longest x68 212 us: apply(): return jnp.einsum(form, table, values, precision=HIGHEST)]
    psum x2 -> x0, blocking collectives: 60.6 us -> none  [local(): flux = lax.psum(jnp.dot(weights, center, precision=HIGHEST), ('vel', 'sub'))]
    all_to_all x6 -> x0, blocking collectives: 55.7 us -> none  [the longest x1 17.2 us: local(): lax.all_to_all(post.reshape(count, count * count, 1, cells), 'vel', split...]
    pallas_call x0 -> x1, Pallas kernels: none -> 49.2 us  [local(): pl.pallas_call(functools.partial(kernel, vel_count, dt, norms), out_shape...]
    slice x25 -> x0, local copies, waits for them, and re-layouts: 23.2 us -> none  [the longest x8 8.34 us: local(): jnp.roll(center, -height_count, 1)]
    all_to_all x13 -> x0, local copies, waits for them, and re-layouts: 19.3 us -> none  [the longest x4 10.1 us: local(): lax.all_to_all(lax.all_to_all(post.reshape(count, count * count, 1, cells...]
    add x3 -> x0, other arithmetic: 17.2 us -> none  [the longest x2 17.1 us: collide(): return cube + rate * (gain - cube * inverse(tables[2]))]
    all_to_all x6 -> x0, other arithmetic: 11.5 us -> none  [the longest x2 4.4 us: local(): lax.all_to_all(lax.all_to_all(post.reshape(count, count * count, 1, cells...]
  transfers between devices with their start and end apart: 4 -> 0, of which waited for: 2 -> 0; matrix products, arithmetic and copies ran while one was open for 7% -> 0% of each run, Pallas kernels for 0% -> 0%
where the time goes in v1:
time: 59.3 us; the launch traced here: 58.9 us
  Pallas kernels  49.2 us (83%)
  local copies, waits for them, and re-layouts  9.66 us (16%)
    pallas_call x1, Pallas kernels, local(): pl.pallas_call(functools.partial(kernel, vel_count, dt, norms), out_shape...  49.2 us
    unnamed x19, local copies, waits for them, and re-layouts  9.66 us

profile of v1, /device:TPU:1, one launch (start us, length us, event | category | flops | bytes accessed | tf_op | source)
XLA Modules:
  0.0 58.9 jit_solution(15568179647724387775)
XLA Ops:
  0.0 0.0 copy-start
  0.0 1.4 %copy-done = f32[3,2,256,256]{3,2,1,0:T(8,128)S(1)} copy-done((f32[3,2,256,256]{3,2,1,0:T(8,128)S(1)}, f32[3,2,256,256]{3,2,1,0:T(8,128)}, u32[]{:S(2)}) %copy-start) | copy-done | bytes 1572888
  1.4 0.0 copy-start.1
  1.4 1.4 %copy-done.1 = bf16[4,768,256]{2,1,0:T(8,128)(2,1)S(1)} copy-done((bf16[4,768,256]{2,1,0:T(8,128)(2,1)S(1)}, bf16[4,768,256]{2,1,0:T(8,128)(2,1)}, u32[]{:S(2)}) %copy-start.1) | copy-done | bytes 1572888
  2.8 0.0 copy-start.2
  2.8 1.0 %copy-done.2 = f32[8,32,512]{2,1,0:T(8,128)S(1)} copy-done((f32[8,32,512]{2,1,0:T(8,128)S(1)}, f32[8,32,512]{2,1,0:T(8,128)}, u32[]{:S(2)}) %copy-start.2) | copy-done | bytes 524312
  3.9 0.0 copy-start.3
  3.9 1.0 %copy-done.3 = f32[3,256,128]{2,1,0:T(8,128)S(1)} copy-done((f32[3,256,128]{2,1,0:T(8,128)S(1)}, f32[3,256,128]{2,1,0:T(8,128)}, u32[]{:S(2)}) %copy-start.3) | copy-done | bytes 393240
  4.9 0.0 copy-start.4
  4.9 1.0 %copy-done.4 = bf16[256,768]{1,0:T(8,128)(2,1)S(1)} copy-done((bf16[256,768]{1,0:T(8,128)(2,1)S(1)}, bf16[256,768]{1,0:T(8,128)(2,1)}, u32[]{:S(2)}) %copy-start.4) | copy-done | bytes 393240
  5.9 0.0 copy-start.5
  5.9 1.0 %copy-done.5 = bf16[256,768]{1,0:T(8,128)(2,1)S(1)} copy-done((bf16[256,768]{1,0:T(8,128)(2,1)S(1)}, bf16[256,768]{1,0:T(8,128)(2,1)}, u32[]{:S(2)}) %copy-start.5) | copy-done | bytes 393240
  6.8 0.0 copy-start.6
  6.9 0.7 %copy-done.6 = f32[8,128]{1,0:T(8,128)S(1)} copy-done((f32[8,128]{1,0:T(8,128)S(1)}, f32[8,128]{1,0:T(8,128)}, u32[]{:S(2)}) %copy-start.6) | copy-done | bytes 4120
  7.5 0.0 copy-start.7
  7.5 0.7 %copy-done.7 = s32[512]{0:T(512)S(1)} copy-done((s32[512]{0:T(512)S(1)}, s32[512]{0:T(512)}, u32[]{:S(2)}) %copy-start.7) | copy-done | bytes 2072
  8.2 0.0 copy-start.8
  8.2 0.7 %copy-done.8 = s32[32]{0:T(128)S(1)} copy-done((s32[32]{0:T(128)S(1)}, s32[32]{0:T(128)}, u32[]{:S(2)}) %copy-start.8) | copy-done | bytes 152
  8.9 49.2 %shard_map.91 = f32[8,32,512]{2,1,0:T(8,128)S(1)} custom-call(s32[512]{0:T(512)S(1)} %copy-done.7, s32[32]{0:T(128)S(1)} %copy-done.8, f32[8,32,512]{2,1,0:T(8,128)S(1)} %copy-done.2, bf16[256,768]{1,0:T(8,128)(2,1)S(1)} %copy-done.5, bf16[256,768]{1,0:T(8,128)(2,1)S(1)} %copy-done.4, bf16[4,768,256]{2,1,0:T(8,128)(2,1)S(1)} %copy-done.1, ...), custom_call_target="tpu_custom_call" | custom-call | tf_op jit(solution)/shard_map/pallas_call | solution.py:437
  58.1 0.8 %copy.11 = f32[8,32,512]{2,1,0:T(8,128)} copy(f32[8,32,512]{2,1,0:T(8,128)S(1)} %shard_map.91) | data formatting | bytes 1048576
Async XLA Ops:
  0.0 1.4 %copy-start = (f32[3,2,256,256]{3,2,1,0:T(8,128)S(1)}, f32[3,2,256,256]{3,2,1,0:T(8,128)}, u32[]{:S(2)}) copy-start(f32[3,2,256,256]{3,2,1,0:T(8,128)} %constant.15.clone.tables_hbm) | copy-start | bytes 4718596
  1.4 1.4 %copy-start.1 = (bf16[4,768,256]{2,1,0:T(8,128)(2,1)S(1)}, bf16[4,768,256]{2,1,0:T(8,128)(2,1)}, u32[]{:S(2)}) copy-start(bf16[4,768,256]{2,1,0:T(8,128)(2,1)} %constant.14.clone.height_hbm) | copy-start | bytes 4718596
  2.8 1.0 %copy-start.2 = (f32[8,32,512]{2,1,0:T(8,128)S(1)}, f32[8,32,512]{2,1,0:T(8,128)}, u32[]{:S(2)}) copy-start(f32[8,32,512]{2,1,0:T(8,128)} %dist_ref.1) | copy-start | bytes 1572868
  3.9 1.0 %copy-start.3 = (f32[3,256,128]{2,1,0:T(8,128)S(1)}, f32[3,256,128]{2,1,0:T(8,128)}, u32[]{:S(2)}) copy-start(f32[3,256,128]{2,1,0:T(8,128)} %constant.16.clone.rows_hbm) | copy-start | bytes 1179652
  4.9 1.0 %copy-start.4 = (bf16[256,768]{1,0:T(8,128)(2,1)S(1)}, bf16[256,768]{1,0:T(8,128)(2,1)}, u32[]{:S(2)}) copy-start(bf16[256,768]{1,0:T(8,128)(2,1)} %constant.13.clone.inverse_hbm) | copy-start | bytes 1179652
  5.9 1.0 %copy-start.5 = (bf16[256,768]{1,0:T(8,128)(2,1)S(1)}, bf16[256,768]{1,0:T(8,128)(2,1)}, u32[]{:S(2)}) copy-start(bf16[256,768]{1,0:T(8,128)(2,1)} %constant.12.clone.forward_hbm) | copy-start | bytes 1179652
  6.8 0.7 %copy-start.6 = (f32[8,128]{1,0:T(8,128)S(1)}, f32[8,128]{1,0:T(8,128)}, u32[]{:S(2)}) copy-start(f32[8,128]{1,0:T(8,128)} %constant.17.clone.lanes_ref) | copy-start | bytes 12292
  7.5 0.7 %copy-start.7 = (s32[512]{0:T(512)S(1)}, s32[512]{0:T(512)}, u32[]{:S(2)}) copy-start(s32[512]{0:T(512)} %cell_ref.1) | copy-start | bytes 6148
  8.2 0.7 %copy-start.8 = (s32[32]{0:T(128)S(1)}, s32[32]{0:T(128)}, u32[]{:S(2)}) copy-start(s32[32]{0:T(128)} %groove_ref.1) | copy-start | bytes 388

commit v2 on v1

--- a/solution.py
+++ b/solution.py
@@ -127,13 +127,15 @@
 
 def kernel(
     vel_count, dt, norms,
-    cell_ref, groove_ref, dist_ref, forward_hbm, inverse_hbm, height_hbm, tables_hbm, rows_hbm,
+    cell_ref, groove_ref, dist_hbm, forward_hbm, inverse_hbm, height_hbm, tables_hbm, rows_hbm,
     lanes_ref, out_ref,
-    stage, back, grid, post, gains, halo_out, halo_in, forward, inverse, height, tables, rows,
+    dist_ref, stage, back, grid, post, gains, halo_out, halo_in, forward, inverse, height, tables, rows,
     table_sem, own_sem, send_sem, recv_sem, halo_send, halo_recv, back_send, back_recv,
 ):
     devices = 2 * vel_count
     depth = dist_ref.shape[1]
+    fetch = pltpu.make_async_copy(dist_hbm, dist_ref, own_sem.at[2])
+    fetch.start()
     group = lax.axis_index("groups")
     vel = lax.axis_index("vel")
     sub = lax.axis_index("sub")
@@ -173,12 +175,20 @@
         )
 
     pl.semaphore_wait(barrier, devices - 1)
+    fetch.wait()
 
     lane = lax.broadcasted_iota(jnp.int32, (1, LANES), 1)
     low_pair = lane < 64
     even_chunk = lane % 64 < 32
     first_column = lane % CHUNK < SY
     level = lane % SY
+
+    blocks = devices // 4
+    mine = me // 4
+
+    def far_first(turn):
+        ahead = 1 - 2 * (mine % 2)
+        return (mine + ahead * (1 + turn) + 2 * blocks) % blocks
 
     def outward(position):
         return pltpu.make_async_remote_copy(
@@ -192,7 +202,7 @@
 
     @pl.loop(0, devices // 4)
     def _(turn):
-        block = (turn + me // 4) % (devices // 4)
+        block = far_first(turn)
         start = pl.multiple_of(block * LANES, LANES)
         for part in range(2):
             pieces = []
@@ -380,9 +390,14 @@
             device_id_type=MESH,
         )
 
-    @pl.loop(1, devices)
-    def _(offset):
-        homeward((me + offset) % devices).start()
+    @pl.loop(0, blocks)
+    def _(turn):
+        for index in range(4):
+            position = 4 * far_first(turn) + index
+
+            @pl.when(position != me)
+            def _():
+                homeward(position).start()
 
     own_back = pltpu.make_async_copy(
         grid.at[pl.ds(2 * sub, 2), pl.ds(vel * depth, depth), :], back.at[me], own_sem.at[1]
@@ -437,9 +452,10 @@
         return pl.pallas_call(
             functools.partial(kernel, vel_count, dt, norms),
             out_shape=jax.ShapeDtypeStruct(dist.shape, F32),
-            in_specs=[smem, smem, vmem, hbm, hbm, hbm, hbm, hbm, vmem],
+            in_specs=[smem, smem, hbm, hbm, hbm, hbm, hbm, hbm, vmem],
             out_specs=vmem,
             scratch_shapes=[
+                pltpu.VMEM(dist.shape, F32),
                 pltpu.VMEM((devices,) + piece, F32),
                 pltpu.VMEM((devices,) + piece, F32),
                 pltpu.VMEM((4, PLANE, LANES), F32),
@@ -453,7 +469,7 @@
                 pltpu.VMEM(tables.shape, F32),
                 pltpu.VMEM(rows.shape, F32),
                 dma((5,)),
-                dma((2,)),
+                dma((3,)),
                 dma((devices,)),
                 dma((devices,)),
                 dma((2 * STEPS,)),
@@ -462,7 +478,7 @@
                 dma((devices,)),
             ],
             compiler_params=pltpu.CompilerParams(
-                collective_id=0, has_side_effects=True, vmem_limit_bytes=40 * 1024 * 1024
+                collective_id=0, has_side_effects=True, vmem_limit_bytes=60 * 1024 * 1024
             ),
         )(
             cell_type, groove_mask, dist,

time: 59.3 us -> 50.7 us (0.85)
  local copies, waits for them, and re-layouts: 9.66 us -> 1.87 us
    unnamed x19 -> x1, local copies, waits for them, and re-layouts: 9.66 us -> 1.87 us
where the time goes in v2:
time: 50.7 us; the launch traced here: 50.6 us
  Pallas kernels  48.7 us (96%)
  local copies, waits for them, and re-layouts  1.87 us (4%)
    pallas_call x1, Pallas kernels, local(): pl.pallas_call(functools.partial(kernel, vel_count, dt, norms), out_shape...  48.7 us
    unnamed x1, local copies, waits for them, and re-layouts  1.87 us

profile of v2, /device:TPU:1, one launch (start us, length us, event | category | flops | bytes accessed | tf_op | source)
XLA Modules:
  0.0 50.6 jit_solution(8884130776417101453)
XLA Ops:
  0.0 48.7 %shard_map.91 = f32[8,32,512]{2,1,0:T(8,128)} custom-call(s32[512]{0:T(512)} %cell_ref.1, s32[32]{0:T(128)} %groove_ref.1, f32[8,32,512]{2,1,0:T(8,128)} %dist_hbm.1, bf16[256,768]{1,0:T(8,128)(2,1)} %constant.12.clone.forward_hbm, bf16[256,768]{1,0:T(8,128)(2,1)} %constant.13.clone.inverse_hbm, bf16[4,768,256]{2,1,0:T(8,128)(2,1)} %constant.14.clone.height_hbm, ...), custom_call_target="tpu_custom_call" | custom-call | tf_op jit(solution)/shard_map/pallas_call | solution.py:452
  48.7 1.9 %copy.11 = f32[8,32,512]{2,1,0:T(8,128)} copy(f32[8,32,512]{2,1,0:T(8,128)} %shard_map.91) | data formatting | bytes 1048576

commit v3 on v2

v3 whole, which is shorter than its diff:
```python
import functools
import math

import jax
import jax.numpy as jnp
import numpy as np
from jax import lax
from jax.experimental import pallas as pl
from jax.experimental.pallas import tpu as pltpu
from jax.sharding import PartitionSpec as P

VN = 16
SY = 16
STEPS = 2

VEL_RANGE = 5.0
TOP_SPEED = 1.0
ACC_LAND = 0.4
ACC_TOP = 0.7
KNUDSEN = 1.0
HALF = VN // 2
PLANE = VN * VN
LANES = 128
MESH = pl.DeviceIdType.MESH
F32 = jnp.float32
BF16 = jnp.bfloat16


def real_basis():
    place = np.arange(VN) - (VN - 1) / 2.0
    modes = np.concatenate([np.arange(HALF), np.arange(1, HALF + 1)])
    rows = []
    for index, mode in enumerate(modes):
        angle = 2.0 * math.pi * mode * place / VN
        row = np.cos(angle) if index < HALF else np.sin(angle)
        rows.append(row / np.sqrt(np.sum(row * row)))
    return modes, np.stack(rows)


def halves(table):
    high = table.astype(np.float32).astype(jnp.bfloat16)
    low = (table - high.astype(np.float64)).astype(jnp.bfloat16)
    return high, low


def left_table(table):
    high, low = halves(table)
    return np.concatenate([high, high, low], axis=1)


def right_table(table):
    high, low = halves(table)
    return np.concatenate([high, high, low], axis=0)


@functools.cache
def constants():
    modes, basis = real_basis()
    step = 2.0 * VEL_RANGE / VN
    plane = np.kron(basis, basis)
    order = np.concatenate([np.arange(HALF), np.arange(VN - 1, HALF - 1, -1)])
    across = np.kron(basis[:, order].T, np.eye(SY))
    forward = left_table(plane)
    inverse = left_table(plane.T)
    height = np.stack([right_table(across), right_table(across.T)])
    wave = modes * (math.pi / VEL_RANGE)
    along_y = wave[:, None, None]
    along_x = wave[None, :, None]
    along_z = wave[None, None, :]
    square = along_y**2 + along_x**2 + along_z**2
    first = 1.0 / (1.0 + square / 12.0)
    second = 3.0 * np.cos(0.9 * along_x) / (1.0 + square / 10.0)
    loss = 3.0 / (1.0 + square / 9.0) ** 2
    tables = []
    for table in (first, second, loss):
        tables.append(np.repeat(table.reshape(VN, PLANE).T, SY, axis=1))
    tables = np.stack(tables).astype(np.float32)

    speed = (np.arange(VN) - (VN - 1) / 2.0) * step
    dt = 0.8 / ((VN - 1) * step)
    gauss = np.exp(-speed * speed / 2.0)
    moving = np.exp(-((speed - TOP_SPEED) ** 2) / 2.0)
    speed_x = np.repeat(speed, VN)
    rows = np.stack([np.abs(speed_x), np.kron(gauss, gauss), np.kron(moving, gauss)])
    rows = np.broadcast_to(rows[:, :, None], (3, PLANE, LANES)).astype(np.float32)
    lanes = np.zeros((8, LANES))
    lanes[0] = np.repeat(np.abs(speed[:HALF]), SY)
    lanes[1] = np.repeat(gauss[:HALF], SY)
    up = np.sum(np.maximum(speed, 0.0) * gauss)
    total = np.sum(gauss)
    norms = (
        up * total * total,
        up * total * total,
        up * total * total,
        up * np.sum(moving) * total,
    )
    return forward, inverse, height, tables, rows, lanes.astype(np.float32), dt, norms


def roll(value, shift):
    return pltpu.roll(value, shift % LANES, 1)


def chunk_transpose(parts, lane):
    parts = list(parts)
    for bit in (4, 2, 1):
        width = bit * SY
        first = lane % (2 * width) < width
        for index in range(HALF):
            if index & bit == 0:
                a, b = parts[index], parts[index + bit]
                parts[index] = jnp.where(first, a, roll(b, width))
                parts[index + bit] = jnp.where(first, roll(a, -width), b)
    return parts


def split(value):
    high = value.astype(BF16)
    low = (value - high.astype(F32)).astype(BF16)
    return high, low


def kernel(
    vel_count, dt, norms,
    cell_ref, groove_ref, dist_hbm, forward_hbm, inverse_hbm, height_hbm, tables_hbm, rows_hbm,
    lanes_ref, out_ref,
    dist_ref, stage, back, grid, post, gains, halo_in, forward, inverse, height, tables, rows,
    table_sem, own_sem, send_sem, recv_sem, halo_send, halo_recv, back_send, back_recv,
):
    devices = 2 * vel_count
    depth = dist_ref.shape[1]
    fetch = pltpu.make_async_copy(dist_hbm, dist_ref, own_sem.at[4])
    fetch.start()
    group = lax.axis_index("groups")
    vel = lax.axis_index("vel")
    sub = lax.axis_index("sub")
    ring = vel // 2 + (vel % 2) * (vel_count - 1 - 2 * (vel // 2))
    me = 2 * ring + sub

    def place_of(position):
        index = position // 2
        far = index // (vel_count // 2)
        return 2 * index + far * (2 * (vel_count - 1 - index) + 1 - 2 * index), position % 2

    def device_of(position):
        v, s = place_of(position)
        return (group, v, s)

    loads = [
        pltpu.make_async_copy(source, target, table_sem.at[index])
        for index, (source, target) in enumerate(
            (
                (forward_hbm, forward),
                (inverse_hbm, inverse),
                (height_hbm, height),
                (tables_hbm, tables),
                (rows_hbm, rows),
            )
        )
    ]
    for load in loads:
        load.start()

    barrier = pltpu.get_barrier_semaphore()

    @pl.loop(1, devices)
    def _(offset):
        pl.semaphore_signal(
            barrier, inc=1, device_id=device_of((me + offset) % devices), device_id_type=MESH
        )

    pl.semaphore_wait(barrier, devices - 1)
    fetch.wait()

    lane = lax.broadcasted_iota(jnp.int32, (1, LANES), 1)
    level = lane % SY

    blocks = devices // 4
    mine = me // 4

    def far_first(turn):
        ahead = 1 - 2 * (mine % 2)
        return (mine + ahead * (1 + turn) + 2 * blocks) % blocks

    def outward(column, position):
        return pltpu.make_async_remote_copy(
            src_ref=stage.at[column, position],
            dst_ref=grid.at[column, sub, pl.ds(vel * depth, depth), :],
            send_sem=send_sem.at[column, position],
            recv_sem=recv_sem.at[column, me],
            device_id=device_of(position),
            device_id_type=MESH,
        )

    def send_block(column, block, copy_of):
        for index in range(4):
            position = 4 * block + index

            @pl.when(position != me)
            def _():
                copy_of(column, position).start()

    @pl.loop(0, blocks)
    def _(turn):
        block = far_first(turn)
        start = pl.multiple_of(block * LANES, LANES)
        pieces = []
        for m in range(HALF):
            y = m + sub * (HALF - 1 - 2 * m)
            pieces.append(dist_ref[y, :, pl.ds(start, LANES)])
        for index, piece in enumerate(chunk_transpose(pieces, lane)):
            stage[index % 2, 4 * block + index // 2] = piece
        send_block(0, block, outward)

    @pl.loop(0, blocks)
    def _(turn):
        send_block(1, far_first(turn), outward)

    own = [
        pltpu.make_async_copy(
            stage.at[column, me],
            grid.at[column, sub, pl.ds(vel * depth, depth), :],
            own_sem.at[column],
        )
        for column in range(2)
    ]
    for copy in own:
        copy.start()

    def solid_count(column):
        count = jnp.int32(0)
        for index in range(SY):
            count = count + cell_ref[column * SY + index]
        return count

    columns = 2 * devices
    counts = [solid_count((2 * me + shift + columns) % columns) for shift in range(-1, 3)]
    top_wall = level == SY - 1

    for load in loads:
        load.wait()

    def inward(column, source):
        v, s = place_of(source)
        return pltpu.make_async_remote_copy(
            src_ref=stage.at[column, source],
            dst_ref=grid.at[column, s, pl.ds(v * depth, depth), :],
            send_sem=send_sem.at[column, source],
            recv_sem=recv_sem.at[column, source],
            device_id=device_of(source),
            device_id_type=MESH,
        )

    def homeward(column, position):
        v, s = place_of(position)
        return pltpu.make_async_remote_copy(
            src_ref=grid.at[column, s, pl.ds(v * depth, depth), :],
            dst_ref=back.at[column, me],
            send_sem=back_send.at[column, position],
            recv_sem=back_recv.at[column, me],
            device_id=device_of(position),
            device_id_type=MESH,
        )

    rate = dt / KNUDSEN
    right_device = device_of((me + 1) % devices)
    left_device = device_of((me + devices - 1) % devices)

    def by_height(value, index):
        high, low = split(value)
        return jnp.dot(
            jnp.concatenate([high, low, high], axis=1), height[index], preferred_element_type=F32
        )

    def by_plane(table, value):
        high, low = split(value)
        return jnp.dot(
            table[...], jnp.concatenate([high, low, high], axis=0), preferred_element_type=F32
        )

    sides = (slice(0, PLANE // 2), slice(PLANE // 2, PLANE))

    @pl.loop(0, STEPS)
    def _(step):
        fluxes = []
        copies = []
        for column in range(2):

            @pl.when(step == 0)
            def _():
                own[column].wait()

                @pl.loop(1, devices)
                def _(offset):
                    inward(column, (me + devices - offset) % devices).wait_recv()

            whole = jnp.concatenate([grid[column, 0], grid[column, 1]], axis=1)
            spectrum = by_plane(forward, by_height(whole, 0))
            for index in range(3):
                gains[index] = by_height(by_plane(inverse, spectrum * tables[index]), 1)
            flux = [jnp.zeros((1, LANES), F32) for _ in range(4)]
            for side in range(2):
                for half in range(2):
                    part = slice(half * LANES, (half + 1) * LANES)
                    value = grid[column, half, sides[side]]
                    value = value + rate * (
                        gains[0, sides[side], part] * gains[1, sides[side], part]
                        - value * gains[2, sides[side], part]
                    )
                    post[column, half, sides[side]] = value
                    flux[side] = flux[side] + jnp.sum(
                        value * rows[0, sides[side]], axis=0, keepdims=True
                    )
                    flux[2 + half] = flux[2 + half] + lanes_ref[0:1] * jnp.sum(
                        value, axis=0, keepdims=True
                    )
            for index in range(4):
                for width in (64, 32, 16):
                    flux[index] = flux[index] + roll(flux[index], width)
            fluxes.append(flux)
            copy = pltpu.make_async_remote_copy(
                src_ref=post.at[column, :, sides[column], :],
                dst_ref=halo_in.at[2 * step + column],
                send_sem=halo_send.at[2 * step + column],
                recv_sem=halo_recv.at[2 * step + column],
                device_id=left_device if column == 0 else right_device,
                device_id_type=MESH,
            )
            copy.start()
            copies.append(copy)

        speed_y, gauss_y = lanes_ref[0:1], lanes_ref[1:2]
        for column in range(2):
            flux = fluxes[column]
            count = counts[1 + column]
            fluid = jnp.where(level < count, 0.0, 1.0)
            below_solid = level <= count
            groove = groove_ref[2 * me + column]
            accommodation = jnp.where(groove == 1, F32(1.0), F32(ACC_LAND))
            for side in (column, 1 - column):
                solid = level < counts[2 + column if side == 0 else column]
                scale = flux[1 - side] * (gauss_y / norms[1 - side])
                if side != column:
                    copies[side].wait()
                for half in range(2):
                    center = post[column, half, sides[side]]
                    mirror = post[column, 1 - half, sides[side]]
                    if side == column:
                        across = post[1 - column, half, sides[side]]
                    else:
                        across = halo_in[2 * step + side, half]
                    across = jnp.where(solid, rows[1, sides[side]] * scale, across)
                    if half == 0:
                        ghost = (1.0 - ACC_TOP) * mirror + rows[2, sides[side]] * (
                            flux[3] * (gauss_y * (ACC_TOP / norms[3]))
                        )
                        along = jnp.where(top_wall, ghost, roll(center, -1))
                    else:
                        ghost = (1.0 - accommodation) * mirror + rows[1, sides[side]] * (
                            accommodation * flux[2] * (gauss_y / norms[2])
                        )
                        along = jnp.where(below_solid, ghost, roll(center, 1))
                    change = rows[0, sides[side]] * (center - across) + speed_y * (center - along)
                    grid[column, half, sides[side]] = (center - dt * change) * fluid

            @pl.when(step == STEPS - 1)
            def _():
                @pl.loop(0, blocks)
                def _(turn):
                    send_block(column, far_first(turn), homeward)

    own_back = [
        pltpu.make_async_copy(
            grid.at[column, sub, pl.ds(vel * depth, depth), :],
            back.at[column, me],
            own_sem.at[2 + column],
        )
        for column in range(2)
    ]
    for copy in own_back:
        copy.start()
    for column in range(2):

        @pl.loop(1, devices)
        def _(offset):
            outward(column, (me + offset) % devices).wait_send()

    for copy in own_back:
        copy.wait()
    for column in range(2):

        @pl.loop(1, devices)
        def _(offset):
            source = (me + devices - offset) % devices
            pltpu.make_async_remote_copy(
                src_ref=stage.at[column, source],
                dst_ref=back.at[column, source],
                send_sem=back_send.at[column, source],
                recv_sem=back_recv.at[column, source],
                device_id=device_of(source),
                device_id_type=MESH,
            ).wait_recv()

    @pl.loop(0, blocks)
    def _(block):
        start = pl.multiple_of(block * LANES, LANES)
        pieces = [back[index % 2, 4 * block + index // 2] for index in range(HALF)]
        for m, piece in enumerate(chunk_transpose(pieces, lane)):
            y = m + sub * (HALF - 1 - 2 * m)
            out_ref[y, :, pl.ds(start, LANES)] = piece

    for column in range(2):

        @pl.loop(1, devices)
        def _(offset):
            homeward(column, (me + offset) % devices).wait_send()


def solution(mesh):
    vel_count = mesh.shape["vel"]
    devices = 2 * vel_count
    forward, inverse, height, tables, rows, lanes, dt, norms = constants()
    depth = PLANE // vel_count

    def local(dist, cell_type, groove_mask):
        hbm = pl.BlockSpec(memory_space=pl.ANY)
        vmem = pl.BlockSpec(memory_space=pltpu.VMEM)
        smem = pl.BlockSpec(memory_space=pltpu.SMEM)
        dma = pltpu.SemaphoreType.DMA
        piece = (2, devices, depth, LANES)
        return pl.pallas_call(
            functools.partial(kernel, vel_count, dt, norms),
            out_shape=jax.ShapeDtypeStruct(dist.shape, F32),
            in_specs=[smem, smem, hbm, hbm, hbm, hbm, hbm, hbm, vmem],
            out_specs=vmem,
            scratch_shapes=[
                pltpu.VMEM(dist.shape, F32),
                pltpu.VMEM(piece, F32),
                pltpu.VMEM(piece, F32),
                pltpu.VMEM((2, 2, PLANE, LANES), F32),
                pltpu.VMEM((2, 2, PLANE, LANES), F32),
                pltpu.VMEM((3, PLANE, PLANE), F32),
                pltpu.VMEM((2 * STEPS, 2, PLANE // 2, LANES), F32),
                pltpu.VMEM(forward.shape, BF16),
                pltpu.VMEM(inverse.shape, BF16),
                pltpu.VMEM(height.shape, BF16),
                pltpu.VMEM(tables.shape, F32),
                pltpu.VMEM(rows.shape, F32),
                dma((5,)),
                dma((5,)),
                dma((2, devices)),
                dma((2, devices)),
                dma((2 * STEPS,)),
                dma((2 * STEPS,)),
                dma((2, devices)),
                dma((2, devices)),
            ],
            compiler_params=pltpu.CompilerParams(
                collective_id=0, has_side_effects=True, vmem_limit_bytes=60 * 1024 * 1024
            ),
        )(
            cell_type, groove_mask, dist,
            jnp.asarray(forward), jnp.asarray(inverse), jnp.asarray(height),
            jnp.asarray(tables), jnp.asarray(rows), jnp.asarray(lanes),
        )

    return jax.shard_map(
        local,
        mesh=mesh,
        in_specs=(P("sub", "vel", "groups"), P("groups"), P("groups")),
        out_specs=P("sub", "vel", "groups"),
        check_vma=False,
    )
```

time: 50.7 us -> 49.6 us (0.978)
  Pallas kernels: 48.7 us -> 47.2 us
    pallas_call x1, Pallas kernels: 48.7 us -> 47.2 us  [local(): pl.pallas_call(functools.partial(kernel, vel_count, dt, norms), out_shape...]
where the time goes in v3:
time: 49.6 us; the launch traced here: 49.1 us
  Pallas kernels  47.2 us (95%)
  local copies, waits for them, and re-layouts  1.87 us (4%)
    pallas_call x1, Pallas kernels, local(): pl.pallas_call(functools.partial(kernel, vel_count, dt, norms), out_shape...  47.2 us
    unnamed x1, local copies, waits for them, and re-layouts  1.87 us

profile of v3, /device:TPU:1, one launch (start us, length us, event | category | flops | bytes accessed | tf_op | source)
XLA Modules:
  0.0 49.1 jit_solution(9429296328190615847)
XLA Ops:
  0.0 47.2 %shard_map.91 = f32[8,32,512]{2,1,0:T(8,128)} custom-call(s32[512]{0:T(512)} %cell_ref.1, s32[32]{0:T(128)} %groove_ref.1, f32[8,32,512]{2,1,0:T(8,128)} %dist_hbm.1, bf16[256,768]{1,0:T(8,128)(2,1)} %constant.12.clone.forward_hbm, bf16[256,768]{1,0:T(8,128)(2,1)} %constant.13.clone.inverse_hbm, bf16[2,768,256]{2,1,0:T(8,128)(2,1)} %constant.14.clone.height_hbm, ...), custom_call_target="tpu_custom_call" | custom-call | tf_op jit(solution)/shard_map/pallas_call | solution.py:431
  47.2 1.9 %copy.11 = f32[8,32,512]{2,1,0:T(8,128)} copy(f32[8,32,512]{2,1,0:T(8,128)} %shard_map.91) | data formatting | bytes 1048576

commit v4 on v3

--- a/solution.py
+++ b/solution.py
@@ -129,7 +129,7 @@
 ):
     devices = 2 * vel_count
     depth = dist_ref.shape[1]
-    fetch = pltpu.make_async_copy(dist_hbm, dist_ref, own_sem.at[4])
+    fetch = pltpu.make_async_copy(dist_hbm, dist_ref, own_sem.at[0])
     fetch.start()
     group = lax.axis_index("groups")
     vel = lax.axis_index("vel")
@@ -186,17 +186,20 @@
         return pltpu.make_async_remote_copy(
             src_ref=stage.at[column, position],
             dst_ref=grid.at[column, sub, pl.ds(vel * depth, depth), :],
-            send_sem=send_sem.at[column, position],
-            recv_sem=recv_sem.at[column, me],
+            send_sem=send_sem.at[column],
+            recv_sem=recv_sem.at[column],
             device_id=device_of(position),
             device_id_type=MESH,
         )
 
-    def send_block(column, block, copy_of):
+    def send_block(column, block, copy_of, side=None):
         for index in range(4):
             position = 4 * block + index
-
-            @pl.when(position != me)
+            wanted = position != me
+            if side is not None:
+                wanted &= place_of(position)[0] // (vel_count // 2) == side
+
+            @pl.when(wanted)
             def _():
                 copy_of(column, position).start()
 
@@ -220,7 +223,7 @@
         pltpu.make_async_copy(
             stage.at[column, me],
             grid.at[column, sub, pl.ds(vel * depth, depth), :],
-            own_sem.at[column],
+            recv_sem.at[column],
         )
         for column in range(2)
     ]
@@ -240,24 +243,13 @@
     for load in loads:
         load.wait()
 
-    def inward(column, source):
-        v, s = place_of(source)
-        return pltpu.make_async_remote_copy(
-            src_ref=stage.at[column, source],
-            dst_ref=grid.at[column, s, pl.ds(v * depth, depth), :],
-            send_sem=send_sem.at[column, source],
-            recv_sem=recv_sem.at[column, source],
-            device_id=device_of(source),
-            device_id_type=MESH,
-        )
-
     def homeward(column, position):
         v, s = place_of(position)
         return pltpu.make_async_remote_copy(
             src_ref=grid.at[column, s, pl.ds(v * depth, depth), :],
             dst_ref=back.at[column, me],
-            send_sem=back_send.at[column, position],
-            recv_sem=back_recv.at[column, me],
+            send_sem=back_send.at[column],
+            recv_sem=back_recv.at[column],
             device_id=device_of(position),
             device_id_type=MESH,
         )
@@ -288,11 +280,7 @@
 
             @pl.when(step == 0)
             def _():
-                own[column].wait()
-
-                @pl.loop(1, devices)
-                def _(offset):
-                    inward(column, (me + devices - offset) % devices).wait_recv()
+                pltpu.make_async_copy(grid.at[column], grid.at[column], recv_sem.at[column]).wait()
 
             whole = jnp.concatenate([grid[column, 0], grid[column, 1]], axis=1)
             spectrum = by_plane(forward, by_height(whole, 0))
@@ -330,76 +318,52 @@
             copies.append(copy)
 
         speed_y, gauss_y = lanes_ref[0:1], lanes_ref[1:2]
-        for column in range(2):
+        for column, side in ((0, 0), (1, 1), (1, 0), (0, 1)):
             flux = fluxes[column]
             count = counts[1 + column]
             fluid = jnp.where(level < count, 0.0, 1.0)
             below_solid = level <= count
             groove = groove_ref[2 * me + column]
             accommodation = jnp.where(groove == 1, F32(1.0), F32(ACC_LAND))
-            for side in (column, 1 - column):
-                solid = level < counts[2 + column if side == 0 else column]
-                scale = flux[1 - side] * (gauss_y / norms[1 - side])
-                if side != column:
-                    copies[side].wait()
-                for half in range(2):
-                    center = post[column, half, sides[side]]
-                    mirror = post[column, 1 - half, sides[side]]
-                    if side == column:
-                        across = post[1 - column, half, sides[side]]
-                    else:
-                        across = halo_in[2 * step + side, half]
-                    across = jnp.where(solid, rows[1, sides[side]] * scale, across)
-                    if half == 0:
-                        ghost = (1.0 - ACC_TOP) * mirror + rows[2, sides[side]] * (
-                            flux[3] * (gauss_y * (ACC_TOP / norms[3]))
-                        )
-                        along = jnp.where(top_wall, ghost, roll(center, -1))
-                    else:
-                        ghost = (1.0 - accommodation) * mirror + rows[1, sides[side]] * (
-                            accommodation * flux[2] * (gauss_y / norms[2])
-                        )
-                        along = jnp.where(below_solid, ghost, roll(center, 1))
-                    change = rows[0, sides[side]] * (center - across) + speed_y * (center - along)
-                    grid[column, half, sides[side]] = (center - dt * change) * fluid
+            solid = level < counts[2 + column if side == 0 else column]
+            scale = flux[1 - side] * (gauss_y / norms[1 - side])
+            if side != column:
+                copies[side].wait()
+            for half in range(2):
+                center = post[column, half, sides[side]]
+                mirror = post[column, 1 - half, sides[side]]
+                if side == column:
+                    across = post[1 - column, half, sides[side]]
+                else:
+                    across = halo_in[2 * step + side, half]
+                across = jnp.where(solid, rows[1, sides[side]] * scale, across)
+                if half == 0:
+                    ghost = (1.0 - ACC_TOP) * mirror + rows[2, sides[side]] * (
+                        flux[3] * (gauss_y * (ACC_TOP / norms[3]))
+                    )
+                    along = jnp.where(top_wall, ghost, roll(center, -1))
+                else:
+                    ghost = (1.0 - accommodation) * mirror + rows[1, sides[side]] * (
+                        accommodation * flux[2] * (gauss_y / norms[2])
+                    )
+                    along = jnp.where(below_solid, ghost, roll(center, 1))
+                change = rows[0, sides[side]] * (center - across) + speed_y * (center - along)
+                grid[column, half, sides[side]] = (center - dt * change) * fluid
 
             @pl.when(step == STEPS - 1)
             def _():
                 @pl.loop(0, blocks)
                 def _(turn):
-                    send_block(column, far_first(turn), homeward)
-
-    own_back = [
+                    send_block(column, far_first(turn), homeward, side)
+
+    for column in range(2):
         pltpu.make_async_copy(
             grid.at[column, sub, pl.ds(vel * depth, depth), :],
             back.at[column, me],
-            own_sem.at[2 + column],
-        )
-        for column in range(2)
-    ]
-    for copy in own_back:
-        copy.start()
+            back_recv.at[column],
+        ).start()
     for column in range(2):
-
-        @pl.loop(1, devices)
-        def _(offset):
-            outward(column, (me + offset) % devices).wait_send()
-
-    for copy in own_back:
-        copy.wait()
-    for column in range(2):
-
-        @pl.loop(1, devices)
-        def _(offset):
-            source = (me + devices - offset) % devices
-            pltpu.make_async_remote_copy(
-                src_ref=stage.at[column, source],
-                dst_ref=back.at[column, source],
-                send_sem=back_send.at[column, source],
-                recv_sem=back_recv.at[column, source],
-                device_id=device_of(source),
-                device_id_type=MESH,
-            ).wait_recv()
+        pltpu.make_async_copy(back.at[column], back.at[column], back_recv.at[column]).wait()
 
     @pl.loop(0, blocks)
     def _(block):
@@ -410,10 +374,9 @@
             out_ref[y, :, pl.ds(start, LANES)] = piece
 
     for column in range(2):
-
-        @pl.loop(1, devices)
-        def _(offset):
-            homeward(column, (me + offset) % devices).wait_send()
+        for sem in (send_sem, back_send):
+            sent = stage.at[column, pl.ds(0, devices - 1)]
+            pltpu.make_async_copy(sent, sent, sem.at[column]).wait()
 
 
 def solution(mesh):
@@ -447,13 +410,13 @@
                 pltpu.VMEM(tables.shape, F32),
                 pltpu.VMEM(rows.shape, F32),
                 dma((5,)),
-                dma((5,)),
-                dma((2, devices)),
-                dma((2, devices)),
+                dma((1,)),
+                dma((2,)),
+                dma((2,)),
                 dma((2 * STEPS,)),
                 dma((2 * STEPS,)),
-                dma((2, devices)),
-                dma((2, devices)),
+                dma((2,)),
+                dma((2,)),
             ],
             compiler_params=pltpu.CompilerParams(
                 collective_id=0, has_side_effects=True, vmem_limit_bytes=60 * 1024 * 1024

time: 49.6 us -> 46.6 us (0.940)
  Pallas kernels: 47.2 us -> 44.2 us
    pallas_call x1, Pallas kernels: 47.2 us -> 44.2 us  [local(): pl.pallas_call(functools.partial(kernel, vel_count, dt, norms), out_shape...]
where the time goes in v4:
time: 46.6 us; the launch traced here: 46.1 us
  Pallas kernels  44.2 us (95%)
  local copies, waits for them, and re-layouts  1.87 us (4%)
    pallas_call x1, Pallas kernels, local(): pl.pallas_call(functools.partial(kernel, vel_count, dt, norms), out_shape...  44.2 us
    unnamed x1, local copies, waits for them, and re-layouts  1.87 us

profile of v4, /device:TPU:1, one launch (start us, length us, event | category | flops | bytes accessed | tf_op | source)
XLA Modules:
  0.0 46.1 jit_solution(12185792898449038668)
XLA Ops:
  0.0 44.2 %shard_map.91 = f32[8,32,512]{2,1,0:T(8,128)} custom-call(s32[512]{0:T(512)} %cell_ref.1, s32[32]{0:T(128)} %groove_ref.1, f32[8,32,512]{2,1,0:T(8,128)} %dist_hbm.1, bf16[256,768]{1,0:T(8,128)(2,1)} %constant.12.clone.forward_hbm, bf16[256,768]{1,0:T(8,128)(2,1)} %constant.13.clone.inverse_hbm, bf16[2,768,256]{2,1,0:T(8,128)(2,1)} %constant.14.clone.height_hbm, ...), custom_call_target="tpu_custom_call" | custom-call | tf_op jit(solution)/shard_map/pallas_call | solution.py:394
  44.3 1.9 %copy.11 = f32[8,32,512]{2,1,0:T(8,128)} copy(f32[8,32,512]{2,1,0:T(8,128)} %shard_map.91) | data formatting | bytes 1048576

commit v5 on v4

--- a/solution.py
+++ b/solution.py
@@ -169,7 +169,6 @@
             barrier, inc=1, device_id=device_of((me + offset) % devices), device_id_type=MESH
         )
 
-    pl.semaphore_wait(barrier, devices - 1)
     fetch.wait()
 
     lane = lax.broadcasted_iota(jnp.int32, (1, LANES), 1)
@@ -203,7 +202,7 @@
             def _():
                 copy_of(column, position).start()
 
-    @pl.loop(0, blocks)
+    @pl.loop(0, blocks, unroll=4)
     def _(turn):
         block = far_first(turn)
         start = pl.multiple_of(block * LANES, LANES)
@@ -213,11 +212,13 @@
             pieces.append(dist_ref[y, :, pl.ds(start, LANES)])
         for index, piece in enumerate(chunk_transpose(pieces, lane)):
             stage[index % 2, 4 * block + index // 2] = piece
-        send_block(0, block, outward)
-
-    @pl.loop(0, blocks)
-    def _(turn):
-        send_block(1, far_first(turn), outward)
+
+    pl.semaphore_wait(barrier, devices - 1)
+    for column in range(2):
+
+        @pl.loop(0, blocks)
+        def _(turn):
+            send_block(column, far_first(turn), outward)
 
     own = [
         pltpu.make_async_copy(
@@ -365,7 +366,7 @@
     for column in range(2):
         pltpu.make_async_copy(back.at[column], back.at[column], back_recv.at[column]).wait()
 
-    @pl.loop(0, blocks)
+    @pl.loop(0, blocks, unroll=4)
     def _(block):
         start = pl.multiple_of(block * LANES, LANES)
         pieces = [back[index % 2, 4 * block + index // 2] for index in range(HALF)]

time: 46.6 us -> 46.2 us (level)
  no operation moved by 1% of the time
where the time goes in v5:
time: 46.2 us; the launch traced here: 45.7 us
  Pallas kernels  43.8 us (95%)
  local copies, waits for them, and re-layouts  1.87 us (4%)
    pallas_call x1, Pallas kernels, local(): pl.pallas_call(functools.partial(kernel, vel_count, dt, norms), out_shape...  43.8 us
    unnamed x1, local copies, waits for them, and re-layouts  1.87 us

profile of v5, /device:TPU:1, one launch (start us, length us, event | category | flops | bytes accessed | tf_op | source)
XLA Modules:
  0.0 45.7 jit_solution(11671980095687507676)
XLA Ops:
  0.0 43.8 %shard_map.91 = f32[8,32,512]{2,1,0:T(8,128)} custom-call(s32[512]{0:T(512)} %cell_ref.1, s32[32]{0:T(128)} %groove_ref.1, f32[8,32,512]{2,1,0:T(8,128)} %dist_hbm.1, bf16[256,768]{1,0:T(8,128)(2,1)} %constant.12.clone.forward_hbm, bf16[256,768]{1,0:T(8,128)(2,1)} %constant.13.clone.inverse_hbm, bf16[2,768,256]{2,1,0:T(8,128)(2,1)} %constant.14.clone.height_hbm, ...), custom_call_target="tpu_custom_call" | custom-call | tf_op jit(solution)/shard_map/pallas_call | solution.py:395
  43.8 1.9 %copy.11 = f32[8,32,512]{2,1,0:T(8,128)} copy(f32[8,32,512]{2,1,0:T(8,128)} %shard_map.91) | data formatting | bytes 1048576
